TPU v7x, 32 devices: a whole 2x2x4 slice. The times are simulated.
32 devices in a mesh: rep: 2 (over y), blk: 8 (over z, x), sub: 2 (over core).
Axes of the slice: x: 2, y: 2, z: 4, core: 2. Of those that a mesh axis runs over, the one named last changes fastest.
Arguments:
- queries: float32 [32, 4096], P(('rep', 'blk', 'sub')), parts along dimension 0, may hold values from -0.5 to 0.5
- passages: float32 [32, 4096], P(('rep', 'blk', 'sub')), parts along dimension 0, may hold values from -0.5 to 0.5
- positive: int32 [32], P(('rep', 'blk', 'sub')), parts along dimension 0, may hold values from 0 to 15, each once
Outputs:
- pair_loss: float32 [32], P(('rep', 'blk', 'sub')), parts along dimension 0
- grad_queries: float32 [32, 4096], P(('rep', 'blk', 'sub')), parts along dimension 0
- grad_passages: float32 [32, 4096], P(('rep', 'blk', 'sub')), parts along dimension 0
There are 2 independent parts, one for each index of `rep`. A program takes and returns all parts, laid end to end along the dimension named above; each array names one. Nothing has to cross between parts.
All inputs are finite; a program needn't handle non-finite values.
Results may differ from a plain program's by a relative error of at most 0.0068.
Values may be sent and summed in bfloat16 or wider, within the bound.
A program may use at most 64 MiB of HBM per device.

v0:
```python
import functools

import jax
import jax.numpy as jnp
from jax import lax
from jax.experimental import pallas as pl
from jax.experimental.pallas import tpu as pltpu
from jax.sharding import PartitionSpec as P

score_scale = 50.0
MESH = pl.DeviceIdType.MESH
FOLD = 16


def merged(shard, axis, combine):
    everything = jax.tree.map(lambda part: lax.all_gather(part, axis), shard)
    first = jax.tree.map(lambda part: part[0], everything)

    def step(k, so_far):
        return combine(so_far, jax.tree.map(lambda part: part[k], everything))

    return lax.fori_loop(1, lax.axis_size(axis), step, first)


def against(left, right):
    return lax.dot_general(
        left, right, (((1,), (1,)), ((), ())), preferred_element_type=jnp.float32
    )


def combine_columns(earlier, later):
    top = jnp.maximum(earlier[0], later[0])
    total = earlier[1] * jnp.exp(earlier[0] - top) + later[1] * jnp.exp(later[0] - top)
    return (top, total)


def spread(queries, passages, positive):
    row_count = queries.shape[0]
    group = lax.axis_size("blk") * lax.axis_size("sub")
    pair_count = row_count * group
    start_row = lax.axis_index(("blk", "sub")) * row_count
    query_low = queries.astype(jnp.bfloat16)
    passage_low = passages.astype(jnp.bfloat16)
    all_pass = lax.all_gather(passage_low, ("blk", "sub"), axis=0, tiled=True)
    all_query, all_positive = (
        lax.all_gather(query_low, ("blk", "sub"), axis=0, tiled=True),
        lax.all_gather(positive, ("blk", "sub"), axis=0, tiled=True),
    )
    row_scores = score_scale * against(query_low, all_pass)
    columns = jnp.arange(pair_count, dtype=jnp.int32)
    row_mask = (positive[:, None] == columns[None, :]).astype(jnp.float32)
    row_top = jnp.max(row_scores, axis=1)
    row_lse = row_top + jnp.log(jnp.sum(jnp.exp(row_scores - row_top[:, None]), axis=1))
    pos_score = jnp.sum(row_scores * row_mask, axis=1)
    own_columns = start_row + jnp.arange(row_count, dtype=jnp.int32)
    col_mask = (all_positive[:, None] == own_columns[None, :]).astype(jnp.float32)
    part_top = jnp.max(row_scores, axis=0)
    part_total = jnp.sum(jnp.exp(row_scores - part_top[None, :]), axis=0)
    col_top, col_total = merged((part_top, part_total), ("blk", "sub"), combine_columns)
    col_lse_all = col_top + jnp.log(col_total)
    col_scores = score_scale * against(all_query, passage_low)
    all_row_lse = lax.all_gather(row_lse, ("blk", "sub"), axis=0, tiled=True)
    own_col_lse = lax.dynamic_slice_in_dim(col_lse_all, start_row, row_count, 0)
    pair_loss = 0.5 * (row_lse + jnp.sum(row_mask * col_lse_all[None, :], axis=1)) - pos_score
    row_weights = (
        0.5 * (jnp.exp(row_scores - row_lse[:, None]) + jnp.exp(row_scores - col_lse_all[None, :]))
        - row_mask
    )
    row_weights = row_weights.astype(jnp.bfloat16)
    grad_queries = score_scale * jnp.dot(row_weights, all_pass, preferred_element_type=jnp.float32)
    col_weights = (
        0.5
        * (jnp.exp(col_scores - all_row_lse[:, None]) + jnp.exp(col_scores - own_col_lse[None, :]))
        - col_mask
    )
    col_weights = col_weights.astype(jnp.bfloat16)
    grad_passages = score_scale * lax.dot_general(
        col_weights, all_query, (((0,), (0,)), ((), ())), preferred_element_type=jnp.float32
    )
    return (pair_loss, grad_queries, grad_passages)


def split3(x):
    high = x.astype(jnp.bfloat16)
    rest = x - high.astype(jnp.float32)
    mid = rest.astype(jnp.bfloat16)
    low = (rest - mid.astype(jnp.float32)).astype(jnp.bfloat16)
    return [high, mid, low]


def finish(pairs, me, both, pos, pos_of, loss_ref, grad_q_ref, grad_p_ref):
    width = both.shape[-1]
    flat = pairs * FOLD
    query = both[:, 0:FOLD, :].reshape(flat, width)
    passage = both[:, FOLD : 2 * FOLD, :].reshape(flat, width)

    row_of = lax.broadcasted_iota(jnp.int32, (flat, flat), 0)
    lane_of = lax.broadcasted_iota(jnp.int32, (flat, flat), 1)
    same_place = (row_of & (FOLD - 1)) == (lane_of & (FOLD - 1))
    block_ones = jnp.where(
        (row_of >> 4) == (lane_of >> 4), 1.0, 0.0
    ).astype(jnp.bfloat16)

    def folded(left, right):
        grid = jnp.where(same_place, against(left, right), 0.0)
        return jnp.sum(grid.reshape(pairs, FOLD, flat), axis=1)

    rows = split3(folded(query, passage))
    cols = split3(folded(passage, query))
    sums = jnp.dot(
        jnp.concatenate(rows + cols, axis=0), block_ones, preferred_element_type=jnp.float32
    )

    def part(k):
        return sums[k * pairs : (k + 1) * pairs]

    scores = score_scale * (part(0) + (part(1) + part(2)))
    scores_t = score_scale * (part(3) + (part(4) + part(5)))

    sub = lax.broadcasted_iota(jnp.int32, (pairs, flat), 0)
    own = sub == me

    def down(x):
        top = jnp.max(x, axis=0, keepdims=True)
        return top + jnp.log(jnp.sum(jnp.exp(x - top), axis=0, keepdims=True))

    def across(x):
        top = jnp.max(x, axis=1, keepdims=True)
        total = jnp.sum(jnp.exp(x - top), axis=1, keepdims=True) * (1.0 / FOLD)
        return top + jnp.log(total)

    col_lse_all = down(scores)
    row_lse_all = down(scores_t)
    row = jnp.sum(jnp.where(own, scores, 0.0), axis=0, keepdims=True)
    col = jnp.sum(jnp.where(own, scores_t, 0.0), axis=0, keepdims=True)
    row_lse = across(row)
    col_lse = across(col)

    lane = lax.broadcasted_iota(jnp.int32, (1, flat), 1)
    row_mask = (lane >> 4) == pos
    col_mask = pos_of == me.astype(jnp.float32)
    single = lane == pos * FOLD
    loss = 0.5 * row_lse + jnp.sum(
        jnp.where(single, 0.5 * col_lse_all - row, 0.0), axis=1, keepdims=True
    )
    loss_ref[...] = jnp.broadcast_to(loss, loss_ref.shape)

    row_w = 0.5 * (jnp.exp(row - row_lse) + jnp.exp(row - col_lse_all)) - jnp.where(row_mask, 1.0, 0.0)
    col_w = 0.5 * (jnp.exp(col - row_lse_all) + jnp.exp(col - col_lse)) - jnp.where(col_mask, 1.0, 0.0)

    place = lax.broadcasted_iota(jnp.int32, (FOLD, flat), 0) == (
        lax.broadcasted_iota(jnp.int32, (FOLD, flat), 1) & (FOLD - 1)
    )

    def grad(weights, rows, out_ref):
        wide = jnp.where(place, jnp.broadcast_to(weights, place.shape), 0.0).astype(jnp.bfloat16)
        result = jnp.dot(wide, rows, preferred_element_type=jnp.float32)
        for c in range(FOLD):
            out_ref[0:1, c * width : (c + 1) * width] = result[c : c + 1, :]

    grad(row_w, passage, grad_q_ref)
    grad(col_w, query, grad_p_ref)


def kernel(
    subs, pairs,
    q_ref, p_ref, pos_ref,
    grad_q_ref, grad_p_ref, loss_ref,
    wide, both, places, send_sem, recv_sem, place_send, place_recv,
):
    width = both.shape[-1]
    chips = pairs // subs
    chip, sub = lax.axis_index("blk"), lax.axis_index("sub")
    me = chip * subs + sub
    other = (subs - 1) - sub

    def rows_to(target, source, k):
        return (
            pltpu.make_async_remote_copy(
                src_ref=both.at[source], dst_ref=both.at[source],
                send_sem=send_sem.at[k], recv_sem=recv_sem.at[source],
                device_id=target, device_id_type=MESH,
            ),
            pltpu.make_async_remote_copy(
                src_ref=places.at[source], dst_ref=places.at[source],
                send_sem=place_send.at[k], recv_sem=place_recv.at[source],
                device_id=target, device_id_type=MESH,
            ),
        )

    def over_link(k, source):
        return rows_to({"blk": k, "sub": sub}, source, k)

    def across(k):
        return rows_to({"blk": chip, "sub": other}, k * subs + sub, chips + k)

    def start(copies):
        for copy in copies:
            copy.start()

    def wait_recv(copies):
        for copy in copies:
            copy.wait_recv()

    def wait_send(copies):
        for copy in copies:
            copy.wait_send()

    def each(first, end, body):
        def step(k, carry):
            body(k)
            return carry

        lax.fori_loop(first, end, step, 0)

    barrier = pltpu.get_barrier_semaphore()

    def greet(k):
        pl.semaphore_signal(
            barrier, inc=1, device_id={"blk": k, "sub": sub}, device_id_type=MESH
        )

    each(chip + 1, chips, greet)
    pl.semaphore_signal(
        barrier, inc=1, device_id={"blk": chip, "sub": other}, device_id_type=MESH
    )

    for c in range(FOLD):
        wide[c : c + 1, :] = q_ref[0:1, c * width : (c + 1) * width]
        wide[FOLD + c : FOLD + c + 1, :] = p_ref[0:1, c * width : (c + 1) * width]
    both[me] = wide[...].astype(jnp.bfloat16)
    pos = pos_ref[0]
    places[me] = jnp.full(places.shape[1:], pos.astype(jnp.float32), jnp.float32)

    pl.semaphore_wait(barrier, chip + 1)

    def send(k):
        start(over_link(k, me))

    def hand_on(k):
        wait_recv(over_link(k, k * subs + sub))
        start(across(k))

    def answer(k):
        hand_on(k)
        send(k)

    def receive(k):
        wait_recv(rows_to({"blk": chip, "sub": other}, k * subs + other, chips + k))

    each(0, chip, send)
    start(across(chip))
    each(chip + 1, chips, answer)
    each(0, chip, hand_on)
    each(0, chips, receive)

    lane = lax.broadcasted_iota(jnp.int32, (1, pairs * FOLD), 1)
    pos_of = jnp.zeros((1, pairs * FOLD), jnp.float32)
    for k in range(pairs):
        pos_of = jnp.where((lane >> 4) == k, places[k, 0:1, :], pos_of)

    finish(pairs, me, both[...], pos, pos_of, loss_ref, grad_q_ref, grad_p_ref)

    each(0, chip, lambda k: wait_send(over_link(k, me)))
    each(chip + 1, chips, lambda k: wait_send(over_link(k, me)))
    each(0, chips, lambda k: wait_send(across(k)))


def local(subs, pairs, queries, passages, positive):
    width = queries.shape[1] // FOLD
    vmem = pl.BlockSpec(memory_space=pltpu.VMEM)
    flat = pairs * FOLD
    grad_q, grad_p, loss = pl.pallas_call(
        functools.partial(kernel, subs, pairs),
        out_shape=(
            jax.ShapeDtypeStruct(queries.shape, jnp.float32),
            jax.ShapeDtypeStruct(passages.shape, jnp.float32),
            jax.ShapeDtypeStruct((1, 128), jnp.float32),
        ),
        in_specs=[vmem, vmem, pl.BlockSpec(memory_space=pltpu.SMEM)],
        out_specs=(vmem, vmem, vmem),
        scratch_shapes=[
            pltpu.VMEM((2 * FOLD, width), jnp.float32),
            pltpu.VMEM((pairs, 2 * FOLD, width), jnp.bfloat16),
            pltpu.VMEM((pairs, 1, flat), jnp.float32),
            pltpu.SemaphoreType.DMA((pairs,)),
            pltpu.SemaphoreType.DMA((pairs,)),
            pltpu.SemaphoreType.DMA((pairs,)),
            pltpu.SemaphoreType.DMA((pairs,)),
        ],
        compiler_params=pltpu.CompilerParams(collective_id=0, has_side_effects=True, vmem_limit_bytes=8 * 1024 * 1024),
    )(queries, passages, positive)
    return loss[0, 0:1], score_scale * grad_q, score_scale * grad_p


def solution(mesh):
    in_specs = (
        P(("rep", "blk", "sub"), None),
        P(("rep", "blk", "sub"), None),
        P(("rep", "blk", "sub")),
    )
    out_specs = (
        P(("rep", "blk", "sub")),
        P(("rep", "blk", "sub"), None),
        P(("rep", "blk", "sub"), None),
    )
    subs = mesh.shape["sub"]
    group = mesh.shape["blk"] * subs

    def run(queries, passages, positive):
        if queries.shape[0] == 1 and subs == 2 and group * FOLD <= 256:
            return local(subs, group, queries, passages, positive)
        return spread(queries, passages, positive)

    return jax.shard_map(run, mesh=mesh, in_specs=in_specs, out_specs=out_specs, check_vma=False)
```

profile of v0, /device:TPU:25, one launch (start us, length us, event | category | flops | bytes accessed | tf_op | source)
XLA Modules:
  0.0 18.0 jit_solution(15332374247268609558)
XLA Ops:
  1.3 0.0 copy-start
  1.3 0.7 %copy-done = f32[1,4096]{1,0:T(1,128)S(1)} copy-done((f32[1,4096]{1,0:T(1,128)S(1)}, f32[1,4096]{1,0:T(1,128)}, u32[]{:S(2)}) %copy-start) | copy-done | bytes 16408
  2.0 0.0 copy-start.1
  2.0 0.7 %copy-done.1 = f32[1,4096]{1,0:T(1,128)S(1)} copy-done((f32[1,4096]{1,0:T(1,128)S(1)}, f32[1,4096]{1,0:T(1,128)}, u32[]{:S(2)}) %copy-start.1) | copy-done | bytes 16408
  2.7 13.5 %shard_map.58 = (f32[1,4096]{1,0:T(1,128)S(1)}, f32[1,4096]{1,0:T(1,128)S(1)}, f32[1,128]{1,0:T(1,128)S(1)}) custom-call(f32[1,4096]{1,0:T(1,128)S(1)} %copy-done, f32[1,4096]{1,0:T(1,128)S(1)} %copy-done.1, s32[1]{0:T(128)S(6)} %copy.7.pos_ref), custom_call_target="tpu_custom_call" | custom-call | tf_op jit(solution)/shard_map/pallas_call | solution.py:273
  16.2 0.6 %broadcast_multiply_fusion = (f32[1,4096]{1,0:T(1,128)}, f32[1,4096]{1,0:T(1,128)}) fusion(f32[1,4096]{1,0:T(1,128)S(1)} %get-tuple-element.8, f32[1,4096]{1,0:T(1,128)S(1)} %get-tuple-element.7), kind=kLoop, calls=%fused_computation | loop fusion | flops 8192 | bytes 65536 | tf_op jit(solution)/shard_map/mul | solution.py:293
Async XLA Ops:
  1.3 0.7 %copy-start = (f32[1,4096]{1,0:T(1,128)S(1)}, f32[1,4096]{1,0:T(1,128)}, u32[]{:S(2)}) copy-start(f32[1,4096]{1,0:T(1,128)} %q_ref.1) | copy-start | bytes 49156
  2.0 0.7 %copy-start.1 = (f32[1,4096]{1,0:T(1,128)S(1)}, f32[1,4096]{1,0:T(1,128)}, u32[]{:S(2)}) copy-start(f32[1,4096]{1,0:T(1,128)} %p_ref.1) | copy-start | bytes 49156
where the time goes:
time: 18.3 us; the launch traced here: 18 us
  Pallas kernels  13.5 us (74%)
  between operations  2.46 us (13%)
  local copies, waits for them, and re-layouts  1.43 us (8%)
  other arithmetic  0.65 us (4%)
    pallas_call x1, Pallas kernels, local(): pl.pallas_call(functools.partial(kernel, subs, pairs), out_shape=(jax.Sha...  13.5 us
    unnamed x4, local copies, waits for them, and re-layouts  1.43 us
    mul x1, other arithmetic, local(): return (loss[0, 0:1], score_scale * grad_q, score_scale * grad_p)  0.65 us

commit v1 on v0

--- a/solution.py
+++ b/solution.py
@@ -164,9 +164,9 @@
 
 def kernel(
     subs, pairs,
-    q_ref, p_ref, pos_ref,
+    q_hbm, p_hbm, pos_hbm,
     grad_q_ref, grad_p_ref, loss_ref,
-    wide, both, places, send_sem, recv_sem, place_send, place_recv,
+    q_ref, p_ref, pos_ref, load_sem, ready, wide, both, places, send_sem, recv_sem, place_send, place_recv,
 ):
     width = both.shape[-1]
     chips = pairs // subs
@@ -224,15 +224,30 @@
     pl.semaphore_signal(
         barrier, inc=1, device_id={"blk": chip, "sub": other}, device_id_type=MESH
     )
-
+    q_copy = pltpu.make_async_copy(q_hbm, q_ref, load_sem.at[0])
+    p_copy = pltpu.make_async_copy(p_hbm, p_ref, load_sem.at[1])
+    pos_copy = pltpu.make_async_copy(pos_hbm, pos_ref, load_sem.at[2])
+    pos_copy.start()
+    q_copy.start()
+    p_copy.start()
+
+    pl.semaphore_wait(barrier, chip + 1)
+
+    def tell(k):
+        pl.semaphore_signal(
+            ready.at[chip], inc=1, device_id={"blk": k, "sub": sub}, device_id_type=MESH
+        )
+
+    each(0, chip, tell)
+    pos_copy.wait()
+    pos = pos_ref[0]
+    places[me] = jnp.full(places.shape[1:], pos.astype(jnp.float32), jnp.float32)
+    q_copy.wait()
+    p_copy.wait()
     for c in range(FOLD):
         wide[c : c + 1, :] = q_ref[0:1, c * width : (c + 1) * width]
         wide[FOLD + c : FOLD + c + 1, :] = p_ref[0:1, c * width : (c + 1) * width]
     both[me] = wide[...].astype(jnp.bfloat16)
-    pos = pos_ref[0]
-    places[me] = jnp.full(places.shape[1:], pos.astype(jnp.float32), jnp.float32)
-
-    pl.semaphore_wait(barrier, chip + 1)
 
     def send(k):
         start(over_link(k, me))
@@ -242,7 +257,7 @@
         start(across(k))
 
     def answer(k):
-        hand_on(k)
+        pl.semaphore_wait(ready.at[k], 1)
         send(k)
 
     def receive(k):
@@ -251,6 +266,7 @@
     each(0, chip, send)
     start(across(chip))
     each(chip + 1, chips, answer)
+    each(chip + 1, chips, hand_on)
     each(0, chip, hand_on)
     each(0, chips, receive)
 
@@ -266,20 +282,32 @@
     each(0, chips, lambda k: wait_send(across(k)))
 
 
+def write_out(loss_ref, q_ref, p_ref, loss_out, q_out, p_out):
+    loss_out[...] = loss_ref[0, 0:1]
+    q_out[...] = score_scale * q_ref[...]
+    p_out[...] = score_scale * p_ref[...]
+
+
 def local(subs, pairs, queries, passages, positive):
     width = queries.shape[1] // FOLD
     vmem = pl.BlockSpec(memory_space=pltpu.VMEM)
+    anywhere = pl.BlockSpec(memory_space=pltpu.HBM)
     flat = pairs * FOLD
     grad_q, grad_p, loss = pl.pallas_call(
         functools.partial(kernel, subs, pairs),
         out_shape=(
-            jax.ShapeDtypeStruct(queries.shape, jnp.float32),
-            jax.ShapeDtypeStruct(passages.shape, jnp.float32),
-            jax.ShapeDtypeStruct((1, 128), jnp.float32),
+            pltpu.VMEM(queries.shape, jnp.float32),
+            pltpu.VMEM(passages.shape, jnp.float32),
+            pltpu.VMEM((1, 128), jnp.float32),
         ),
-        in_specs=[vmem, vmem, pl.BlockSpec(memory_space=pltpu.SMEM)],
+        in_specs=[anywhere, anywhere, anywhere],
         out_specs=(vmem, vmem, vmem),
         scratch_shapes=[
+            pltpu.VMEM(queries.shape, jnp.float32),
+            pltpu.VMEM(passages.shape, jnp.float32),
+            pltpu.SMEM((1,), jnp.int32),
+            pltpu.SemaphoreType.DMA((3,)),
+            pltpu.SemaphoreType.REGULAR((pairs // subs,)),
             pltpu.VMEM((2 * FOLD, width), jnp.float32),
             pltpu.VMEM((pairs, 2 * FOLD, width), jnp.bfloat16),
             pltpu.VMEM((pairs, 1, flat), jnp.float32),
@@ -289,8 +317,18 @@
             pltpu.SemaphoreType.DMA((pairs,)),
         ],
         compiler_params=pltpu.CompilerParams(collective_id=0, has_side_effects=True, vmem_limit_bytes=8 * 1024 * 1024),
-    )(queries, passages, positive)
-    return loss[0, 0:1], score_scale * grad_q, score_scale * grad_p
+    )(*(pltpu.with_memory_space_constraint(x, pltpu.HBM) for x in (queries, passages)), positive)
+    return pl.pallas_call(
+        write_out,
+        out_shape=(
+            jax.ShapeDtypeStruct((1,), jnp.float32),
+            jax.ShapeDtypeStruct(queries.shape, jnp.float32),
+            jax.ShapeDtypeStruct(passages.shape, jnp.float32),
+        ),
+        in_specs=[vmem, vmem, vmem],
+        out_specs=(vmem, vmem, vmem),
+        compiler_params=pltpu.CompilerParams(vmem_limit_bytes=8 * 1024 * 1024),
+    )(loss, grad_q, grad_p)
 
 
 def solution(mesh):

time: 18.3 us -> 13.2 us (0.72)
  the two profiles are of different devices: /device:TPU:25 before, /device:TPU:1 now
where the time goes in v1:
time: 13.2 us; the launch traced here: 13 us
  Pallas kernels  11.7 us (89%)
  between operations  1.28 us (10%)
    pallas_call x1, Pallas kernels, local(): pl.pallas_call(functools.partial(kernel, subs, pairs), out_shape=(pltpu.V...  11.1 us
    pallas_call x1, Pallas kernels, local(): pl.pallas_call(write_out, out_shape=(jax.ShapeDtypeStruct((1,), jnp.float...  0.62 us

profile of v1, /device:TPU:1, one launch (start us, length us, event | category | flops | bytes accessed | tf_op | source)
XLA Modules:
  0.0 13.0 jit_solution(4563955380105960267)
XLA Ops:
  1.3 11.1 %shard_map.58 = (f32[1,4096]{1,0:T(1,128)S(1)}, f32[1,4096]{1,0:T(1,128)S(1)}, f32[1,128]{1,0:T(1,128)S(1)}) custom-call(f32[1,4096]{1,0:T(1,128)} %q_hbm.1, f32[1,4096]{1,0:T(1,128)} %p_hbm.1, s32[1]{0:T(128)S(6)} %copy.6.pos_hbm), custom_call_target="tpu_custom_call" | custom-call | tf_op jit(solution)/shard_map/pallas_call | solution.py:296
  12.4 0.6 %shard_map.59 = (f32[1]{0:T(128)}, f32[1,4096]{1,0:T(1,128)}, f32[1,4096]{1,0:T(1,128)}) custom-call(f32[1,128]{1,0:T(1,128)S(1)} %get-tuple-element.6.loss_ref, f32[1,4096]{1,0:T(1,128)S(1)} %get-tuple-element.7.q_ref, f32[1,4096]{1,0:T(1,128)S(1)} %get-tuple-element.8.p_ref), custom_call_target="tpu_custom_call" | custom-call | tf_op jit(solution)/shard_map/pallas_call | solution.py:321

commit v2 on v1

--- a/solution.py
+++ b/solution.py
@@ -88,27 +88,20 @@
     return [high, mid, low]
 
 
-def finish(pairs, me, both, pos, pos_of, loss_ref, grad_q_ref, grad_p_ref):
+def finish(pairs, me, same_place, block_ones, both, pos, pos_of, loss_ref, grad_q_ref, grad_p_ref):
     width = both.shape[-1]
     flat = pairs * FOLD
     query = both[:, 0:FOLD, :].reshape(flat, width)
     passage = both[:, FOLD : 2 * FOLD, :].reshape(flat, width)
 
-    row_of = lax.broadcasted_iota(jnp.int32, (flat, flat), 0)
-    lane_of = lax.broadcasted_iota(jnp.int32, (flat, flat), 1)
-    same_place = (row_of & (FOLD - 1)) == (lane_of & (FOLD - 1))
-    block_ones = jnp.where(
-        (row_of >> 4) == (lane_of >> 4), 1.0, 0.0
-    ).astype(jnp.bfloat16)
-
     def folded(left, right):
-        grid = jnp.where(same_place, against(left, right), 0.0)
+        grid = against(left, right) * same_place[...]
         return jnp.sum(grid.reshape(pairs, FOLD, flat), axis=1)
 
     rows = split3(folded(query, passage))
     cols = split3(folded(passage, query))
     sums = jnp.dot(
-        jnp.concatenate(rows + cols, axis=0), block_ones, preferred_element_type=jnp.float32
+        jnp.concatenate(rows + cols, axis=0), block_ones[...], preferred_element_type=jnp.float32
     )
 
     def part(k):
@@ -166,7 +159,7 @@
     subs, pairs,
     q_hbm, p_hbm, pos_hbm,
     grad_q_ref, grad_p_ref, loss_ref,
-    q_ref, p_ref, pos_ref, load_sem, ready, wide, both, places, send_sem, recv_sem, place_send, place_recv,
+    same_place, block_ones, q_ref, p_ref, pos_ref, load_sem, ready, wide, both, places, send_sem, recv_sem, place_send, place_recv,
 ):
     width = both.shape[-1]
     chips = pairs // subs
@@ -213,23 +206,24 @@
 
         lax.fori_loop(first, end, step, 0)
 
-    barrier = pltpu.get_barrier_semaphore()
-
-    def greet(k):
-        pl.semaphore_signal(
-            barrier, inc=1, device_id={"blk": k, "sub": sub}, device_id_type=MESH
-        )
-
-    each(chip + 1, chips, greet)
-    pl.semaphore_signal(
-        barrier, inc=1, device_id={"blk": chip, "sub": other}, device_id_type=MESH
-    )
     q_copy = pltpu.make_async_copy(q_hbm, q_ref, load_sem.at[0])
     p_copy = pltpu.make_async_copy(p_hbm, p_ref, load_sem.at[1])
     pos_copy = pltpu.make_async_copy(pos_hbm, pos_ref, load_sem.at[2])
     pos_copy.start()
     q_copy.start()
     p_copy.start()
+
+    barrier = pltpu.get_barrier_semaphore()
+
+    def greet(k):
+        pl.semaphore_signal(
+            barrier, inc=1, device_id={"blk": k, "sub": sub}, device_id_type=MESH
+        )
+
+    each(chip + 1, chips, greet)
+    pl.semaphore_signal(
+        barrier, inc=1, device_id={"blk": chip, "sub": other}, device_id_type=MESH
+    )
 
     pl.semaphore_wait(barrier, chip + 1)
 
@@ -266,8 +260,13 @@
     each(0, chip, send)
     start(across(chip))
     each(chip + 1, chips, answer)
+    flat = pairs * FOLD
+    row_of = lax.broadcasted_iota(jnp.int32, (flat, flat), 0)
+    lane_of = lax.broadcasted_iota(jnp.int32, (flat, flat), 1)
+    same_place[...] = jnp.where((row_of & (FOLD - 1)) == (lane_of & (FOLD - 1)), 1.0, 0.0)
+    block_ones[...] = jnp.where((row_of >> 4) == (lane_of >> 4), 1.0, 0.0).astype(jnp.bfloat16)
+    each(0, chip, hand_on)
     each(chip + 1, chips, hand_on)
-    each(0, chip, hand_on)
     each(0, chips, receive)
 
     lane = lax.broadcasted_iota(jnp.int32, (1, pairs * FOLD), 1)
@@ -275,7 +274,7 @@
     for k in range(pairs):
         pos_of = jnp.where((lane >> 4) == k, places[k, 0:1, :], pos_of)
 
-    finish(pairs, me, both[...], pos, pos_of, loss_ref, grad_q_ref, grad_p_ref)
+    finish(pairs, me, same_place, block_ones, both[...], pos, pos_of, loss_ref, grad_q_ref, grad_p_ref)
 
     each(0, chip, lambda k: wait_send(over_link(k, me)))
     each(chip + 1, chips, lambda k: wait_send(over_link(k, me)))
@@ -303,6 +302,8 @@
         in_specs=[anywhere, anywhere, anywhere],
         out_specs=(vmem, vmem, vmem),
         scratch_shapes=[
+            pltpu.VMEM((flat, flat), jnp.float32),
+            pltpu.VMEM((flat, flat), jnp.bfloat16),
             pltpu.VMEM(queries.shape, jnp.float32),
             pltpu.VMEM(passages.shape, jnp.float32),
             pltpu.SMEM((1,), jnp.int32),

time: 13.2 us -> 13.2 us (level)
  no operation moved by 1% of the time
where the time goes in v2:
time: 13.2 us; the launch traced here: 12.9 us
  Pallas kernels  11.6 us (88%)
  between operations  1.28 us (10%)
    pallas_call x1, Pallas kernels, local(): pl.pallas_call(functools.partial(kernel, subs, pairs), out_shape=(pltpu.V...  11 us
    pallas_call x1, Pallas kernels, local(): pl.pallas_call(write_out, out_shape=(jax.ShapeDtypeStruct((1,), jnp.float...  0.62 us

profile of v2, /device:TPU:1, one launch (start us, length us, event | category | flops | bytes accessed | tf_op | source)
XLA Modules:
  0.0 12.9 jit_solution(17411969290438519577)
XLA Ops:
  1.3 11.0 %shard_map.58 = (f32[1,4096]{1,0:T(1,128)S(1)}, f32[1,4096]{1,0:T(1,128)S(1)}, f32[1,128]{1,0:T(1,128)S(1)}) custom-call(f32[1,4096]{1,0:T(1,128)} %q_hbm.1, f32[1,4096]{1,0:T(1,128)} %p_hbm.1, s32[1]{0:T(128)S(6)} %copy.6.pos_hbm), custom_call_target="tpu_custom_call" | custom-call | tf_op jit(solution)/shard_map/pallas_call | solution.py:295
  12.3 0.6 %shard_map.59 = (f32[1]{0:T(128)}, f32[1,4096]{1,0:T(1,128)}, f32[1,4096]{1,0:T(1,128)}) custom-call(f32[1,128]{1,0:T(1,128)S(1)} %get-tuple-element.6.loss_ref, f32[1,4096]{1,0:T(1,128)S(1)} %get-tuple-element.7.q_ref, f32[1,4096]{1,0:T(1,128)S(1)} %get-tuple-element.8.p_ref), custom_call_target="tpu_custom_call" | custom-call | tf_op jit(solution)/shard_map/pallas_call | solution.py:322
